TPU v7x, 32 devices: a whole 2x2x4 slice. The times are simulated.
32 devices in a mesh: shot: 2 (over x), tile: 16 (over z, y, core).
Axes of the slice: x: 2, y: 2, z: 4, core: 2. Of those that a mesh axis runs over, the one named last changes fastest.
Arguments:
- source: bfloat16 [16, 512, 4, 384], P('shot', 'tile'), parts along dimension 0, may hold values from -6 to 6
- receiver: bfloat16 [16, 512, 4, 384], P('shot', 'tile'), parts along dimension 0, may hold values from -6 to 6
- offsets: int32 [64], replicated, may hold values from -32 to 32, as said below
- snap_index: int32 [4], replicated, may hold values from 0 to 7, as said below
Outputs:
- image_lags: float32 [128, 512, 4, 384], P('shot', 'tile'), parts along dimension 0
There are 2 independent parts, one for each index of `shot`. A program takes and returns all parts, laid end to end along the dimension named above; an argument that names none is the same for every part. Nothing has to cross between parts.
Inputs may be any that keep to these rules, and one draw needn't show every extreme that they name: `offsets`: distinct values; the lags -32 and 32 are always present. `snap_index`: distinct values; snapshots 0 and 7 are always present.
All inputs are finite; a program needn't handle non-finite values.
Results may differ from a plain program's by a relative error of at most 0.0003.
Values may be sent and summed in bfloat16 or wider, within the bound.
A program may use at most 192 MiB of HBM per device.

v0:
```python
import functools

import jax
import jax.numpy as jnp
from jax import lax
from jax.experimental import pallas as pl
from jax.experimental.pallas import tpu as pltpu
from jax.sharding import PartitionSpec as P

HMAX = 32
LANES = 128
SUB = 8
MESH = pl.DeviceIdType.MESH


def exchange_kernel(tiles, used, snap_ref, src_ref, rec_ref, left_ref, right_ref, picked, send_sem, recv_sem):
    me = lax.axis_index("tile")
    has_left, has_right = me > 0, me < tiles - 1
    barrier = pltpu.get_barrier_semaphore()

    @pl.when(has_left)
    def _():
        pl.semaphore_signal(barrier, inc=1, device_id={"tile": me - 1}, device_id_type=MESH)

    @pl.when(has_right)
    def _():
        pl.semaphore_signal(barrier, inc=1, device_id={"tile": me + 1}, device_id_type=MESH)

    def up(snap):
        return pltpu.make_async_remote_copy(
            src_ref=picked.at[snap],
            dst_ref=left_ref.at[snap],
            send_sem=send_sem.at[0, snap],
            recv_sem=recv_sem.at[0, snap],
            device_id={"tile": me + 1},
            device_id_type=MESH,
        )

    def down(snap):
        return pltpu.make_async_remote_copy(
            src_ref=picked.at[snap],
            dst_ref=right_ref.at[snap],
            send_sem=send_sem.at[1, snap],
            recv_sem=recv_sem.at[1, snap],
            device_id={"tile": me - 1},
            device_id_type=MESH,
        )

    for snap in range(used):
        picked[snap, 0] = src_ref[snap_ref[snap]]
        picked[snap, 1] = rec_ref[snap_ref[snap]]
        if snap == 0:
            pl.semaphore_wait(barrier, has_left.astype(jnp.int32) + has_right.astype(jnp.int32))

        @pl.when(has_right)
        def _():
            up(snap).start()

        @pl.when(has_left)
        def _():
            down(snap).start()

    for snap in range(used):
        @pl.when(has_right)
        def _():
            up(snap).wait_send()
            down(snap).wait_recv()

        @pl.when(has_left)
        def _():
            down(snap).wait_send()
            up(snap).wait_recv()


def image_kernel(
    tiles, used, lags, cell_rows,
    offset_ref, snap_ref, src_ref, rec_ref, left_ref, right_ref, out_ref,
    raw, fields, image, slot_ref, in_sem, out_sem,
):
    me = lax.axis_index("tile")
    cells, cy, nz = src_ref.shape[1:]
    blocks = nz // LANES
    rows = cells * cell_rows
    pairs = cells // 2
    step = 2 * cell_rows
    base = HMAX * cell_rows

    def lanes(block):
        return pl.ds(block * LANES, LANES)

    own, sides = [], []
    for block in range(blocks):
        for snap in range(used):
            for field, ref in enumerate((src_ref, rec_ref)):
                own.append(pltpu.make_async_copy(
                    ref.at[snap_ref[snap], :, :, lanes(block)],
                    raw.at[1, snap, field, :, block], in_sem.at[1, block, snap, field]))
        for place, ref in ((0, left_ref), (2, right_ref)):
            sides.append(pltpu.make_async_copy(
                ref.at[:, :, :, :, lanes(block)], raw.at[place, :, :, :, block], in_sem.at[place, block, 0, 0]))
    for copy in own + sides:
        copy.start()

    for index in range(2 * HMAX + 1):
        slot_ref[index] = -1
    for lag in range(lags):
        slot_ref[offset_ref[lag] + HMAX] = lag

    def widen(place):
        def body(snap, carry):
            for field in range(2):
                value = raw.at[place, snap, field].reshape(rows, LANES)[...].astype(jnp.float32)
                if field == 0:
                    value = value * ((snap + 1).astype(jnp.float32) / used)
                fields[field, snap, pl.ds(place * rows, rows), :] = value
            return carry
        lax.fori_loop(0, used, body, 0)

    def clear(place):
        def body(snap, carry):
            for field in range(2):
                fields[field, snap, pl.ds(place * rows, rows), :] = jnp.zeros((rows, LANES), jnp.float32)
            return carry
        lax.fori_loop(0, used, body, 0)

    for copy in own:
        copy.wait()
    widen(1)
    for copy in sides:
        copy.wait()
    for place, edge in ((0, me == 0), (2, me == tiles - 1)):
        pl.when(edge)(functools.partial(clear, place))
        pl.when(jnp.logical_not(edge))(functools.partial(widen, place))

    def send(index, slot):
        for block in range(blocks):
            pltpu.make_async_copy(
                image.at[index, :, block], out_ref.at[slot, :, :, lanes(block)], out_sem).start()

    def group(first, odd, width):
        def one_class(part, carry):
            inner = part * SUB
            cache = {}

            def source(place):
                start = base + inner + step * (place - first) - cell_rows * odd
                start = pl.multiple_of(start, 4)
                return [fields[0, snap, pl.ds(start, SUB), :] for snap in range(used)]

            def receiver(place):
                if place not in cache:
                    start = base + inner + step * (place + first) + cell_rows * odd
                    start = pl.multiple_of(start, 4)
                    cache[place] = [fields[1, snap, pl.ds(start, SUB), :] for snap in range(used)]
                return cache[place]

            for place in range(-(width - 1), pairs):
                held = source(place)
                for late in range(width):
                    pair = place + late
                    if 0 <= pair < pairs:
                        other = receiver(place + 2 * late)
                        total = held[0] * other[0]
                        for snap in range(1, used):
                            total = total + held[snap] * other[snap]
                        index = 2 * (first + late) + odd + HMAX
                        sheet = image.at[index].reshape(rows, LANES)
                        sheet[pl.ds(pl.multiple_of(step * pair + inner, SUB), SUB), :] = total
            return carry

        lax.fori_loop(0, step // SUB, one_class, 0)
        for late in range(width):
            index = 2 * (first + late) + odd + HMAX
            slot = slot_ref[index]

            @pl.when(slot >= 0)
            def _():
                send(index, slot)

    def even_groups(number, carry):
        group(3 * number - HMAX // 2, 0, 3)
        return carry

    def odd_groups(number, carry):
        group(4 * number - HMAX // 2, 1, 4)
        return carry

    lax.fori_loop(0, (HMAX + 1) // 3, even_groups, 0)
    lax.fori_loop(0, HMAX // 4, odd_groups, 0)
    for block in range(blocks):
        pltpu.make_async_copy(
            image.at[pl.ds(0, lags), :, block], out_ref.at[:, :, :, lanes(block)], out_sem).wait()


def local(tiles, source, receiver, offsets, snap_index):
    stored, cells, cy, nz = source.shape
    used, lags = snap_index.shape[0], offsets.shape[0]
    cell_rows = cy * nz // LANES
    rows = cells * cell_rows
    assert cells == HMAX and (2 * cell_rows) % SUB == 0
    halo = jax.ShapeDtypeStruct((used, 2, cells, cy, nz), source.dtype)
    vmem = pl.BlockSpec(memory_space=pltpu.VMEM)
    smem = pl.BlockSpec(memory_space=pltpu.SMEM)
    anywhere = pl.BlockSpec(memory_space=pl.ANY)
    left, right = pl.pallas_call(
        functools.partial(exchange_kernel, tiles, used),
        out_shape=(halo, halo),
        in_specs=[smem, vmem, vmem],
        out_specs=(anywhere, anywhere),
        scratch_shapes=[
            pltpu.VMEM((used, 2, cells, cy, nz), source.dtype),
            pltpu.SemaphoreType.DMA((2, used)),
            pltpu.SemaphoreType.DMA((2, used)),
        ],
        compiler_params=pltpu.CompilerParams(
            collective_id=0, has_side_effects=True, vmem_limit_bytes=16 << 20),
    )(snap_index, source, receiver)
    return pl.pallas_call(
        functools.partial(image_kernel, tiles, used, lags, cell_rows),
        out_shape=jax.ShapeDtypeStruct((lags, cells, cy, nz), jnp.float32),
        in_specs=[smem, smem, anywhere, anywhere, anywhere, anywhere],
        out_specs=anywhere,
        scratch_shapes=[
            pltpu.VMEM((3, used, 2, cells, nz // LANES, cy, LANES), source.dtype),
            pltpu.VMEM((2, used, 3 * rows, LANES), jnp.float32),
            pltpu.VMEM((2 * HMAX + 1, cells, nz // LANES, cy, LANES), jnp.float32),
            pltpu.SMEM((2 * HMAX + 1,), jnp.int32),
            pltpu.SemaphoreType.DMA((3, nz // LANES, used, 2)),
            pltpu.SemaphoreType.DMA(()),
        ],
        compiler_params=pltpu.CompilerParams(vmem_limit_bytes=40 << 20),
    )(offsets, snap_index, source, receiver, left, right)


def solution(mesh):
    return jax.shard_map(
        functools.partial(local, mesh.shape["tile"]),
        mesh=mesh,
        in_specs=(P("shot", "tile", None, None), P("shot", "tile", None, None), P(), P()),
        out_specs=P("shot", "tile", None, None),
        check_vma=False,
    )
```

profile of v0, /device:TPU:9, one launch (start us, length us, event | category | flops | bytes accessed | tf_op | source)
XLA Modules:
  0.0 36.5 jit_solution(3696678053359977296)
XLA Ops:
  0.0 0.0 copy-start
  0.0 1.1 %copy-done = bf16[8,32,4,384]{3,2,1,0:T(4,128)(2,1)S(1)} copy-done((bf16[8,32,4,384]{3,2,1,0:T(4,128)(2,1)S(1)}, bf16[8,32,4,384]{3,2,1,0:T(4,128)(2,1)}, u32[]{:S(2)}) %copy-start) | copy-done | bytes 786456
  1.1 0.0 copy-start.2
  1.1 1.1 %copy-done.2 = bf16[8,32,4,384]{3,2,1,0:T(4,128)(2,1)S(1)} copy-done((bf16[8,32,4,384]{3,2,1,0:T(4,128)(2,1)S(1)}, bf16[8,32,4,384]{3,2,1,0:T(4,128)(2,1)}, u32[]{:S(2)}) %copy-start.2) | copy-done | bytes 786456
  2.3 0.0 copy-start.4
  2.3 0.7 %copy-done.4 = s32[4]{0:T(128)S(1)} copy-done((s32[4]{0:T(128)S(1)}, s32[4]{0:T(128)}, u32[]{:S(2)}) %copy-start.4) | copy-done | bytes 40
  2.9 20.7 %shard_map.46 = (bf16[4,2,32,4,384]{4,3,2,1,0:T(4,128)(2,1)S(1)}, bf16[4,2,32,4,384]{4,3,2,1,0:T(4,128)(2,1)S(1)}) custom-call(s32[4]{0:T(128)S(1)} %copy-done.4, bf16[8,32,4,384]{3,2,1,0:T(4,128)(2,1)S(1)} %copy-done, bf16[8,32,4,384]{3,2,1,0:T(4,128)(2,1)S(1)} %copy-done.2), custom_call_target="tpu_custom_call" | custom-call | tf_op jit(solution)/shard_map/pallas_call | solution.py:205
  23.6 0.0 copy-start.1
  23.6 1.1 %copy-done.1 = bf16[8,32,4,384]{3,2,1,0:T(4,128)(2,1)S(1)} copy-done((bf16[8,32,4,384]{3,2,1,0:T(4,128)(2,1)S(1)}, bf16[8,32,4,384]{3,2,1,0:T(4,128)(2,1)}, u32[]{:S(2)}) %copy-start.1) | copy-done | bytes 786456
  24.7 0.0 copy-start.3
  24.7 1.1 %copy-done.3 = bf16[8,32,4,384]{3,2,1,0:T(4,128)(2,1)S(1)} copy-done((bf16[8,32,4,384]{3,2,1,0:T(4,128)(2,1)S(1)}, bf16[8,32,4,384]{3,2,1,0:T(4,128)(2,1)}, u32[]{:S(2)}) %copy-start.3) | copy-done | bytes 786456
  25.9 0.0 copy-start.5
  25.9 0.7 %copy-done.5 = s32[4]{0:T(128)S(1)} copy-done((s32[4]{0:T(128)S(1)}, s32[4]{0:T(128)}, u32[]{:S(2)}) %copy-start.5) | copy-done | bytes 40
  26.5 0.0 copy-start.6
  26.5 0.7 %copy-done.6 = s32[64]{0:T(128)S(1)} copy-done((s32[64]{0:T(128)S(1)}, s32[64]{0:T(128)}, u32[]{:S(2)}) %copy-start.6) | copy-done | bytes 280
  27.2 9.3 %shard_map.47 = f32[64,32,4,384]{3,2,1,0:T(4,128)} custom-call(s32[64]{0:T(128)S(1)} %copy-done.6, s32[4]{0:T(128)S(1)} %copy-done.5, bf16[8,32,4,384]{3,2,1,0:T(4,128)(2,1)S(1)} %copy-done.1, bf16[8,32,4,384]{3,2,1,0:T(4,128)(2,1)S(1)} %copy-done.3, bf16[4,2,32,4,384]{4,3,2,1,0:T(4,128)(2,1)S(1)} %get-tuple-element.7.left_ref, ...), custom_call_target="tpu_custom_call" | custom-call | tf_op jit(solution)/shard_map/pallas_call | solution.py:218
Async XLA Ops:
  0.0 1.1 %copy-start = (bf16[8,32,4,384]{3,2,1,0:T(4,128)(2,1)S(1)}, bf16[8,32,4,384]{3,2,1,0:T(4,128)(2,1)}, u32[]{:S(2)}) copy-start(bf16[8,32,4,384]{3,2,1,0:T(4,128)(2,1)} %src_ref.3) | copy-start | bytes 2359300
  1.1 1.1 %copy-start.2 = (bf16[8,32,4,384]{3,2,1,0:T(4,128)(2,1)S(1)}, bf16[8,32,4,384]{3,2,1,0:T(4,128)(2,1)}, u32[]{:S(2)}) copy-start(bf16[8,32,4,384]{3,2,1,0:T(4,128)(2,1)} %rec_ref.3) | copy-start | bytes 2359300
  2.3 0.7 %copy-start.4 = (s32[4]{0:T(128)S(1)}, s32[4]{0:T(128)}, u32[]{:S(2)}) copy-start(s32[4]{0:T(128)} %snap_ref.3) | copy-start | bytes 52
  23.6 1.1 %copy-start.1 = (bf16[8,32,4,384]{3,2,1,0:T(4,128)(2,1)S(1)}, bf16[8,32,4,384]{3,2,1,0:T(4,128)(2,1)}, u32[]{:S(2)}) copy-start(bf16[8,32,4,384]{3,2,1,0:T(4,128)(2,1)} %src_ref.3) | copy-start | bytes 2359300
  24.7 1.1 %copy-start.3 = (bf16[8,32,4,384]{3,2,1,0:T(4,128)(2,1)S(1)}, bf16[8,32,4,384]{3,2,1,0:T(4,128)(2,1)}, u32[]{:S(2)}) copy-start(bf16[8,32,4,384]{3,2,1,0:T(4,128)(2,1)} %rec_ref.3) | copy-start | bytes 2359300
  25.9 0.7 %copy-start.5 = (s32[4]{0:T(128)S(1)}, s32[4]{0:T(128)}, u32[]{:S(2)}) copy-start(s32[4]{0:T(128)} %snap_ref.3) | copy-start | bytes 52
  26.5 0.7 %copy-start.6 = (s32[64]{0:T(128)S(1)}, s32[64]{0:T(128)}, u32[]{:S(2)}) copy-start(s32[64]{0:T(128)} %offset_ref.1) | copy-start | bytes 772
where the time goes:
time: 36.9 us; the launch traced here: 36.5 us
  Pallas kernels  30 us (81%)
  local copies, waits for them, and re-layouts  6.49 us (18%)
    pallas_call x1, Pallas kernels, local(): pl.pallas_call(functools.partial(exchange_kernel, tiles, used), out_shape...  20.7 us
    pallas_call x1, Pallas kernels, local(): pl.pallas_call(functools.partial(image_kernel, tiles, used, lags, cell_ro...  9.34 us
    unnamed x14, local copies, waits for them, and re-layouts  6.49 us

commit v1 on v0

v1 whole, which is shorter than its diff:
```python
import functools

import jax
import jax.numpy as jnp
from jax import lax
from jax.experimental import pallas as pl
from jax.experimental.pallas import tpu as pltpu
from jax.sharding import PartitionSpec as P

HMAX = 32
LANES = 128
SUB = 8
MESH = pl.DeviceIdType.MESH


def lag_group(fields, cell_rows, pairs, first, odd, width, put):
    step = 2 * cell_rows
    base = HMAX * cell_rows

    def one_class(part, carry):
        inner = part * SUB
        cache = {}

        def source(place):
            start = base + inner + step * (place - first) - cell_rows * odd
            return fields[0, pl.ds(pl.multiple_of(start, 4), SUB), :]

        def receiver(place):
            if place not in cache:
                start = base + inner + step * (place + first) + cell_rows * odd
                cache[place] = fields[1, pl.ds(pl.multiple_of(start, 4), SUB), :]
            return cache[place]

        for place in range(-(width - 1), pairs):
            held = source(place)
            for late in range(width):
                pair = place + late
                if 0 <= pair < pairs:
                    index = 2 * (first + late) + odd + HMAX
                    rows = pl.ds(pl.multiple_of(step * pair + inner, SUB), SUB)
                    put(index, rows, held * receiver(place + 2 * late))
        return carry

    lax.fori_loop(0, step // SUB, one_class, 0)


def exchange_kernel(
    tiles, used, cell_rows, snap_ref, src_ref, rec_ref, partial_ref, last_ref,
    stage, picked, halo, fields, in_sem, send_sem, recv_sem,
):
    me = lax.axis_index("tile")
    has_left, has_right = me > 0, me < tiles - 1
    stored, cells, cy, nz = src_ref.shape
    blocks = nz // LANES
    rows = cells * cell_rows
    barrier = pltpu.get_barrier_semaphore()

    @pl.when(has_left)
    def _():
        pl.semaphore_signal(barrier, inc=1, device_id={"tile": me - 1}, device_id_type=MESH)

    @pl.when(has_right)
    def _():
        pl.semaphore_signal(barrier, inc=1, device_id={"tile": me + 1}, device_id_type=MESH)

    loads = [
        pltpu.make_async_copy(
            ref.at[:, :, :, pl.ds(block * LANES, LANES)], stage.at[field, :, :, block], in_sem.at[field, block])
        for field, ref in enumerate((src_ref, rec_ref))
        for block in range(blocks)
    ]
    for copy in loads:
        copy.start()

    def up(snap):
        return pltpu.make_async_remote_copy(
            src_ref=picked.at[snap],
            dst_ref=halo.at[0, snap],
            send_sem=send_sem.at[0, snap],
            recv_sem=recv_sem.at[0, snap],
            device_id={"tile": me + 1},
            device_id_type=MESH,
        )

    def down(snap):
        return pltpu.make_async_remote_copy(
            src_ref=picked.at[snap],
            dst_ref=halo.at[1, snap],
            send_sem=send_sem.at[1, snap],
            recv_sem=recv_sem.at[1, snap],
            device_id={"tile": me - 1},
            device_id_type=MESH,
        )

    for copy in loads:
        copy.wait()
    rowwise = stage.reshape(2, stored, rows, LANES)
    for snap in range(used):
        for field in range(2):
            picked[snap, field] = rowwise[field, snap_ref[snap]]
        if snap == 0:
            pl.semaphore_wait(barrier, has_left.astype(jnp.int32) + has_right.astype(jnp.int32))

        @pl.when(has_right)
        def _():
            up(snap).start()

        @pl.when(has_left)
        def _():
            down(snap).start()

    def clear(place):
        for field in range(2):
            for ref in (fields, last_ref):
                ref[field, pl.ds(place * rows, rows), :] = jnp.zeros((rows, LANES), jnp.float32)

    pl.when(jnp.logical_not(has_left))(functools.partial(clear, 0))
    pl.when(jnp.logical_not(has_right))(functools.partial(clear, 2))

    def zero(index, carry):
        partial_ref[index] = jnp.zeros((rows, LANES), jnp.float32)
        return carry

    lax.fori_loop(0, 2 * HMAX + 1, zero, 0)

    def widen(target, place, value, field, snap):
        value = value.astype(jnp.float32)
        if field == 0:
            value = value * ((snap + 1).astype(jnp.float32) / used)
        target[field, pl.ds(place * rows, rows), :] = value

    def gather(target, snap):
        for field in range(2):
            widen(target, 1, picked[snap, field], field, snap)

        @pl.when(has_left)
        def _():
            up(snap).wait_recv()
            for field in range(2):
                widen(target, 0, halo[0, snap, field], field, snap)

        @pl.when(has_right)
        def _():
            down(snap).wait_recv()
            for field in range(2):
                widen(target, 2, halo[1, snap, field], field, snap)

    def put(index, where, term):
        partial_ref[index, where, :] += term

    def add(snap, carry):
        gather(fields, snap)

        def even_groups(number, inner):
            lag_group(fields, cell_rows, cells // 2, 11 * number - HMAX // 2, 0, 11, put)
            return inner

        def odd_groups(number, inner):
            lag_group(fields, cell_rows, cells // 2, 8 * number - HMAX // 2, 1, 8, put)
            return inner

        lax.fori_loop(0, (HMAX + 1) // 11, even_groups, 0)
        lax.fori_loop(0, HMAX // 8, odd_groups, 0)
        return carry

    lax.fori_loop(0, used - 1, add, 0)
    gather(last_ref, jnp.int32(used - 1))

    for snap in range(used):
        @pl.when(has_right)
        def _():
            up(snap).wait_send()

        @pl.when(has_left)
        def _():
            down(snap).wait_send()


def image_kernel(lags, cell_rows, offset_ref, partial_ref, last_ref, out_ref, image, slot_ref, out_sem):
    cells, cy, nz = out_ref.shape[1:]
    blocks = nz // LANES
    rows = cells * cell_rows

    for index in range(2 * HMAX + 1):
        slot_ref[index] = -1
    for lag in range(lags):
        slot_ref[offset_ref[lag] + HMAX] = lag

    def lanes(block):
        return pl.ds(block * LANES, LANES)

    def put(index, where, term):
        sheet = image.at[index].reshape(rows, LANES)
        sheet[where, :] = partial_ref[index, where, :] + term

    def group(first, odd, width):
        lag_group(last_ref, cell_rows, cells // 2, first, odd, width, put)
        for late in range(width):
            index = 2 * (first + late) + odd + HMAX
            slot = slot_ref[index]

            @pl.when(slot >= 0)
            def _():
                for block in range(blocks):
                    pltpu.make_async_copy(
                        image.at[index, :, block], out_ref.at[slot, :, :, lanes(block)], out_sem).start()

    def even_groups(number, carry):
        group(3 * number - HMAX // 2, 0, 3)
        return carry

    def odd_groups(number, carry):
        group(4 * number - HMAX // 2, 1, 4)
        return carry

    lax.fori_loop(0, (HMAX + 1) // 3, even_groups, 0)
    lax.fori_loop(0, HMAX // 4, odd_groups, 0)
    for block in range(blocks):
        pltpu.make_async_copy(
            image.at[pl.ds(0, lags), :, block], out_ref.at[:, :, :, lanes(block)], out_sem).wait()


def local(tiles, source, receiver, offsets, snap_index):
    stored, cells, cy, nz = source.shape
    used, lags = snap_index.shape[0], offsets.shape[0]
    blocks = nz // LANES
    cell_rows = cy * blocks
    rows = cells * cell_rows
    assert cells == HMAX and (2 * cell_rows) % SUB == 0
    vmem = pl.BlockSpec(memory_space=pltpu.VMEM)
    smem = pl.BlockSpec(memory_space=pltpu.SMEM)
    anywhere = pl.BlockSpec(memory_space=pl.ANY)
    every = 2 * HMAX + 1
    partial, last = pl.pallas_call(
        functools.partial(exchange_kernel, tiles, used, cell_rows),
        out_shape=(
            jax.ShapeDtypeStruct((every, rows, LANES), jnp.float32),
            jax.ShapeDtypeStruct((2, 3 * rows, LANES), jnp.float32),
        ),
        in_specs=[smem, anywhere, anywhere],
        out_specs=(vmem, vmem),
        scratch_shapes=[
            pltpu.VMEM((2, stored, cells, blocks, cy, LANES), source.dtype),
            pltpu.VMEM((used, 2, rows, LANES), source.dtype),
            pltpu.VMEM((2, used, 2, rows, LANES), source.dtype),
            pltpu.VMEM((2, 3 * rows, LANES), jnp.float32),
            pltpu.SemaphoreType.DMA((2, blocks)),
            pltpu.SemaphoreType.DMA((2, used)),
            pltpu.SemaphoreType.DMA((2, used)),
        ],
        compiler_params=pltpu.CompilerParams(
            collective_id=0, has_side_effects=True, vmem_limit_bytes=32 << 20),
    )(snap_index, source, receiver)
    return pl.pallas_call(
        functools.partial(image_kernel, lags, cell_rows),
        out_shape=jax.ShapeDtypeStruct((lags, cells, cy, nz), jnp.float32),
        in_specs=[smem, vmem, vmem],
        out_specs=anywhere,
        scratch_shapes=[
            pltpu.VMEM((every, cells, blocks, cy, LANES), jnp.float32),
            pltpu.SMEM((every,), jnp.int32),
            pltpu.SemaphoreType.DMA(()),
        ],
        compiler_params=pltpu.CompilerParams(vmem_limit_bytes=32 << 20),
    )(offsets, partial, last)


def solution(mesh):
    return jax.shard_map(
        functools.partial(local, mesh.shape["tile"]),
        mesh=mesh,
        in_specs=(P("shot", "tile", None, None), P("shot", "tile", None, None), P(), P()),
        out_specs=P("shot", "tile", None, None),
        check_vma=False,
    )
```

time: 36.9 us -> 31.3 us (0.85)
  local copies, waits for them, and re-layouts: 6.49 us -> 3.57 us
  Pallas kernels: 30 us -> 27.5 us
    unnamed x14 -> x8, local copies, waits for them, and re-layouts: 6.49 us -> 3.57 us
    pallas_call x2, Pallas kernels: 30 us -> 27.5 us  [the longest x1 22.3 us: local(): pl.pallas_call(functools.partial(exchange_kernel, tiles, used, cell_rows)...]
where the time goes in v1:
time: 31.3 us; the launch traced here: 31.1 us
  Pallas kernels  27.5 us (88%)
  local copies, waits for them, and re-layouts  3.57 us (11%)
    pallas_call x1, Pallas kernels, local(): pl.pallas_call(functools.partial(exchange_kernel, tiles, used, cell_rows)...  22.3 us
    pallas_call x1, Pallas kernels, local(): pl.pallas_call(functools.partial(image_kernel, lags, cell_rows), out_shap...  5.21 us
    unnamed x8, local copies, waits for them, and re-layouts  3.57 us

profile of v1, /device:TPU:9, one launch (start us, length us, event | category | flops | bytes accessed | tf_op | source)
XLA Modules:
  0.0 31.1 jit_solution(7140757502629392208)
XLA Ops:
  0.0 0.0 copy-start
  0.0 1.1 %copy-done = bf16[8,32,4,384]{3,2,1,0:T(4,128)(2,1)S(1)} copy-done((bf16[8,32,4,384]{3,2,1,0:T(4,128)(2,1)S(1)}, bf16[8,32,4,384]{3,2,1,0:T(4,128)(2,1)}, u32[]{:S(2)}) %copy-start) | copy-done | bytes 786456
  1.1 0.0 copy-start.1
  1.1 1.1 %copy-done.1 = bf16[8,32,4,384]{3,2,1,0:T(4,128)(2,1)S(1)} copy-done((bf16[8,32,4,384]{3,2,1,0:T(4,128)(2,1)S(1)}, bf16[8,32,4,384]{3,2,1,0:T(4,128)(2,1)}, u32[]{:S(2)}) %copy-start.1) | copy-done | bytes 786456
  2.3 0.0 copy-start.2
  2.3 0.7 %copy-done.2 = s32[4]{0:T(128)S(1)} copy-done((s32[4]{0:T(128)S(1)}, s32[4]{0:T(128)}, u32[]{:S(2)}) %copy-start.2) | copy-done | bytes 40
  2.9 22.3 %shard_map.46 = (f32[65,384,128]{2,1,0:T(8,128)S(1)}, f32[2,1152,128]{2,1,0:T(8,128)S(1)}) custom-call(s32[4]{0:T(128)S(1)} %copy-done.2, bf16[8,32,4,384]{3,2,1,0:T(4,128)(2,1)S(1)} %copy-done, bf16[8,32,4,384]{3,2,1,0:T(4,128)(2,1)S(1)} %copy-done.1), custom_call_target="tpu_custom_call" | custom-call | tf_op jit(solution)/shard_map/pallas_call | solution.py:234
  25.2 0.0 copy-start.3
  25.3 0.6 %copy-done.3 = s32[64]{0:T(128)S(1)} copy-done((s32[64]{0:T(128)S(1)}, s32[64]{0:T(128)}, u32[]{:S(2)}) %copy-start.3) | copy-done | bytes 280
  25.9 5.2 %shard_map.47 = f32[64,32,4,384]{3,2,1,0:T(4,128)} custom-call(s32[64]{0:T(128)S(1)} %copy-done.3, f32[65,384,128]{2,1,0:T(8,128)S(1)} %get-tuple-element.7.partial_ref, f32[2,1152,128]{2,1,0:T(8,128)S(1)} %get-tuple-element.8.last_ref), custom_call_target="tpu_custom_call" | custom-call | tf_op jit(solution)/shard_map/pallas_call | solution.py:254
Async XLA Ops:
  0.0 1.1 %copy-start = (bf16[8,32,4,384]{3,2,1,0:T(4,128)(2,1)S(1)}, bf16[8,32,4,384]{3,2,1,0:T(4,128)(2,1)}, u32[]{:S(2)}) copy-start(bf16[8,32,4,384]{3,2,1,0:T(4,128)(2,1)} %src_ref.1) | copy-start | bytes 2359300
  1.1 1.1 %copy-start.1 = (bf16[8,32,4,384]{3,2,1,0:T(4,128)(2,1)S(1)}, bf16[8,32,4,384]{3,2,1,0:T(4,128)(2,1)}, u32[]{:S(2)}) copy-start(bf16[8,32,4,384]{3,2,1,0:T(4,128)(2,1)} %rec_ref.1) | copy-start | bytes 2359300
  2.3 0.7 %copy-start.2 = (s32[4]{0:T(128)S(1)}, s32[4]{0:T(128)}, u32[]{:S(2)}) copy-start(s32[4]{0:T(128)} %snap_ref.1) | copy-start | bytes 52
  25.2 0.7 %copy-start.3 = (s32[64]{0:T(128)S(1)}, s32[64]{0:T(128)}, u32[]{:S(2)}) copy-start(s32[64]{0:T(128)} %offset_ref.1) | copy-start | bytes 772

commit v2 on v1

--- a/solution.py
+++ b/solution.py
@@ -44,14 +44,28 @@
     lax.fori_loop(0, step // SUB, one_class, 0)
 
 
+def pick_kernel(used, snap_ref, src_ref, rec_ref, picked_ref, sem):
+    blocks = src_ref.shape[3] // LANES
+    copies = [
+        pltpu.make_async_copy(
+            ref.at[snap_ref[snap], :, :, pl.ds(block * LANES, LANES)],
+            picked_ref.at[snap, field, :, block], sem.at[snap, field, block])
+        for snap in range(used)
+        for field, ref in enumerate((src_ref, rec_ref))
+        for block in range(blocks)
+    ]
+    for copy in copies:
+        copy.start()
+    for copy in copies:
+        copy.wait()
+
+
 def exchange_kernel(
-    tiles, used, cell_rows, snap_ref, src_ref, rec_ref, partial_ref, last_ref,
-    stage, picked, halo, fields, in_sem, send_sem, recv_sem,
+    tiles, cell_rows, picked, partial_ref, last_ref, halo, fields, send_sem, recv_sem,
 ):
     me = lax.axis_index("tile")
     has_left, has_right = me > 0, me < tiles - 1
-    stored, cells, cy, nz = src_ref.shape
-    blocks = nz // LANES
+    used, _, cells, blocks, cy, _ = picked.shape
     rows = cells * cell_rows
     barrier = pltpu.get_barrier_semaphore()
 
@@ -62,15 +76,6 @@
     @pl.when(has_right)
     def _():
         pl.semaphore_signal(barrier, inc=1, device_id={"tile": me + 1}, device_id_type=MESH)
-
-    loads = [
-        pltpu.make_async_copy(
-            ref.at[:, :, :, pl.ds(block * LANES, LANES)], stage.at[field, :, :, block], in_sem.at[field, block])
-        for field, ref in enumerate((src_ref, rec_ref))
-        for block in range(blocks)
-    ]
-    for copy in loads:
-        copy.start()
 
     def up(snap):
         return pltpu.make_async_remote_copy(
@@ -92,15 +97,10 @@
             device_id_type=MESH,
         )
 
-    for copy in loads:
-        copy.wait()
-    rowwise = stage.reshape(2, stored, rows, LANES)
+    beside = halo.reshape(2, used, 2, rows, LANES)
+    own = picked.reshape(used, 2, rows, LANES)
+    pl.semaphore_wait(barrier, has_left.astype(jnp.int32) + has_right.astype(jnp.int32))
     for snap in range(used):
-        for field in range(2):
-            picked[snap, field] = rowwise[field, snap_ref[snap]]
-        if snap == 0:
-            pl.semaphore_wait(barrier, has_left.astype(jnp.int32) + has_right.astype(jnp.int32))
-
         @pl.when(has_right)
         def _():
             up(snap).start()
@@ -131,19 +131,19 @@
 
     def gather(target, snap):
         for field in range(2):
-            widen(target, 1, picked[snap, field], field, snap)
+            widen(target, 1, own[snap, field], field, snap)
 
         @pl.when(has_left)
         def _():
             up(snap).wait_recv()
             for field in range(2):
-                widen(target, 0, halo[0, snap, field], field, snap)
+                widen(target, 0, beside[0, snap, field], field, snap)
 
         @pl.when(has_right)
         def _():
             down(snap).wait_recv()
             for field in range(2):
-                widen(target, 2, halo[1, snap, field], field, snap)
+                widen(target, 2, beside[1, snap, field], field, snap)
 
     def put(index, where, term):
         partial_ref[index, where, :] += term
@@ -231,26 +231,31 @@
     smem = pl.BlockSpec(memory_space=pltpu.SMEM)
     anywhere = pl.BlockSpec(memory_space=pl.ANY)
     every = 2 * HMAX + 1
+    picked = pl.pallas_call(
+        functools.partial(pick_kernel, used),
+        out_shape=jax.ShapeDtypeStruct((used, 2, cells, blocks, cy, LANES), source.dtype),
+        in_specs=[smem, anywhere, anywhere],
+        out_specs=vmem,
+        scratch_shapes=[pltpu.SemaphoreType.DMA((used, 2, blocks))],
+        compiler_params=pltpu.CompilerParams(vmem_limit_bytes=62 << 20),
+    )(snap_index, source, receiver)
     partial, last = pl.pallas_call(
-        functools.partial(exchange_kernel, tiles, used, cell_rows),
+        functools.partial(exchange_kernel, tiles, cell_rows),
         out_shape=(
             jax.ShapeDtypeStruct((every, rows, LANES), jnp.float32),
             jax.ShapeDtypeStruct((2, 3 * rows, LANES), jnp.float32),
         ),
-        in_specs=[smem, anywhere, anywhere],
+        in_specs=[vmem],
         out_specs=(vmem, vmem),
         scratch_shapes=[
-            pltpu.VMEM((2, stored, cells, blocks, cy, LANES), source.dtype),
-            pltpu.VMEM((used, 2, rows, LANES), source.dtype),
-            pltpu.VMEM((2, used, 2, rows, LANES), source.dtype),
+            pltpu.VMEM((2, used, 2, cells, blocks, cy, LANES), source.dtype),
             pltpu.VMEM((2, 3 * rows, LANES), jnp.float32),
-            pltpu.SemaphoreType.DMA((2, blocks)),
             pltpu.SemaphoreType.DMA((2, used)),
             pltpu.SemaphoreType.DMA((2, used)),
         ],
         compiler_params=pltpu.CompilerParams(
             collective_id=0, has_side_effects=True, vmem_limit_bytes=32 << 20),
-    )(snap_index, source, receiver)
+    )(picked)
     return pl.pallas_call(
         functools.partial(image_kernel, lags, cell_rows),
         out_shape=jax.ShapeDtypeStruct((lags, cells, cy, nz), jnp.float32),

time: 31.3 us -> 31.3 us (level)
  local copies, waits for them, and re-layouts: 3.57 us -> 1.78 us
  Pallas kernels: 27.5 us -> 29.2 us
    unnamed x8 -> x4, local copies, waits for them, and re-layouts: 3.57 us -> 1.78 us
    pallas_call x1 -> x2, Pallas kernels: 22.3 us -> 24 us  [the longest x1 21.1 us: local(): pl.pallas_call(functools.partial(exchange_kernel, tiles, cell_rows), out_...]
where the time goes in v2:
time: 31.3 us; the launch traced here: 31 us
  Pallas kernels  29.2 us (93%)
  local copies, waits for them, and re-layouts  1.78 us (6%)
    pallas_call x1, Pallas kernels, local(): pl.pallas_call(functools.partial(exchange_kernel, tiles, cell_rows), out_...  21.1 us
    pallas_call x1, Pallas kernels, local(): pl.pallas_call(functools.partial(image_kernel, lags, cell_rows), out_shap...  5.21 us
    pallas_call x1, Pallas kernels, local(): pl.pallas_call(functools.partial(pick_kernel, used), out_shape=jax.ShapeD...  2.84 us
    unnamed x4, local copies, waits for them, and re-layouts  1.78 us

profile of v2, /device:TPU:9, one launch (start us, length us, event | category | flops | bytes accessed | tf_op | source)
XLA Modules:
  0.0 31.0 jit_solution(16250968515908117955)
XLA Ops:
  0.0 2.8 %shard_map.46.picked = bf16[4,2,32,3,4,128]{5,4,3,2,1,0:T(4,128)(2,1)} custom-call(s32[4]{0:T(128)} %snap_ref.1, bf16[8,32,4,384]{3,2,1,0:T(4,128)(2,1)} %src_ref.1, bf16[8,32,4,384]{3,2,1,0:T(4,128)(2,1)} %rec_ref.1), custom_call_target="tpu_custom_call" | custom-call | tf_op jit(solution)/shard_map/pallas_call | solution.py:234
  2.8 0.0 copy-start
  2.9 1.1 %copy-done = bf16[4,2,32,3,4,128]{5,4,3,2,1,0:T(4,128)(2,1)S(1)} copy-done((bf16[4,2,32,3,4,128]{5,4,3,2,1,0:T(4,128)(2,1)S(1)}, bf16[4,2,32,3,4,128]{5,4,3,2,1,0:T(4,128)(2,1)}, u32[]{:S(2)}) %copy-start) | copy-done | bytes 786456
  4.0 21.1 %shard_map.47 = (f32[65,384,128]{2,1,0:T(8,128)S(1)}, f32[2,1152,128]{2,1,0:T(8,128)S(1)}) custom-call(bf16[4,2,32,3,4,128]{5,4,3,2,1,0:T(4,128)(2,1)S(1)} %copy-done), custom_call_target="tpu_custom_call" | custom-call | tf_op jit(solution)/shard_map/pallas_call | solution.py:242
  25.1 0.0 copy-start.1
  25.1 0.6 %copy-done.1 = s32[64]{0:T(128)S(1)} copy-done((s32[64]{0:T(128)S(1)}, s32[64]{0:T(128)}, u32[]{:S(2)}) %copy-start.1) | copy-done | bytes 280
  25.8 5.2 %shard_map.48 = f32[64,32,4,384]{3,2,1,0:T(4,128)} custom-call(s32[64]{0:T(128)S(1)} %copy-done.1, f32[65,384,128]{2,1,0:T(8,128)S(1)} %get-tuple-element.7.partial_ref, f32[2,1152,128]{2,1,0:T(8,128)S(1)} %get-tuple-element.8.last_ref), custom_call_target="tpu_custom_call" | custom-call | tf_op jit(solution)/shard_map/pallas_call | solution.py:259
Async XLA Ops:
  2.8 1.1 %copy-start = (bf16[4,2,32,3,4,128]{5,4,3,2,1,0:T(4,128)(2,1)S(1)}, bf16[4,2,32,3,4,128]{5,4,3,2,1,0:T(4,128)(2,1)}, u32[]{:S(2)}) copy-start(bf16[4,2,32,3,4,128]{5,4,3,2,1,0:T(4,128)(2,1)} %shard_map.46.picked) | copy-start | bytes 2359300
  25.1 0.7 %copy-start.1 = (s32[64]{0:T(128)S(1)}, s32[64]{0:T(128)}, u32[]{:S(2)}) copy-start(s32[64]{0:T(128)} %offset_ref.1) | copy-start | bytes 772

commit v3 on v2

--- a/solution.py
+++ b/solution.py
@@ -44,24 +44,9 @@
     lax.fori_loop(0, step // SUB, one_class, 0)
 
 
-def pick_kernel(used, snap_ref, src_ref, rec_ref, picked_ref, sem):
-    blocks = src_ref.shape[3] // LANES
-    copies = [
-        pltpu.make_async_copy(
-            ref.at[snap_ref[snap], :, :, pl.ds(block * LANES, LANES)],
-            picked_ref.at[snap, field, :, block], sem.at[snap, field, block])
-        for snap in range(used)
-        for field, ref in enumerate((src_ref, rec_ref))
-        for block in range(blocks)
-    ]
-    for copy in copies:
-        copy.start()
-    for copy in copies:
-        copy.wait()
-
-
 def exchange_kernel(
-    tiles, cell_rows, picked, partial_ref, last_ref, halo, fields, send_sem, recv_sem,
+    tiles, cell_rows, snap_ref, src_ref, rec_ref, partial_ref, last_ref,
+    picked, halo, fields, send_sem, recv_sem,
 ):
     me = lax.axis_index("tile")
     has_left, has_right = me > 0, me < tiles - 1
@@ -99,8 +84,13 @@
 
     beside = halo.reshape(2, used, 2, rows, LANES)
     own = picked.reshape(used, 2, rows, LANES)
-    pl.semaphore_wait(barrier, has_left.astype(jnp.int32) + has_right.astype(jnp.int32))
     for snap in range(used):
+        for field, ref in enumerate((src_ref, rec_ref)):
+            for block in range(blocks):
+                picked[snap, field, :, block] = ref[snap_ref[snap], :, :, pl.ds(block * LANES, LANES)]
+        if snap == 0:
+            pl.semaphore_wait(barrier, has_left.astype(jnp.int32) + has_right.astype(jnp.int32))
+
         @pl.when(has_right)
         def _():
             up(snap).start()
@@ -231,23 +221,16 @@
     smem = pl.BlockSpec(memory_space=pltpu.SMEM)
     anywhere = pl.BlockSpec(memory_space=pl.ANY)
     every = 2 * HMAX + 1
-    picked = pl.pallas_call(
-        functools.partial(pick_kernel, used),
-        out_shape=jax.ShapeDtypeStruct((used, 2, cells, blocks, cy, LANES), source.dtype),
-        in_specs=[smem, anywhere, anywhere],
-        out_specs=vmem,
-        scratch_shapes=[pltpu.SemaphoreType.DMA((used, 2, blocks))],
-        compiler_params=pltpu.CompilerParams(vmem_limit_bytes=62 << 20),
-    )(snap_index, source, receiver)
     partial, last = pl.pallas_call(
         functools.partial(exchange_kernel, tiles, cell_rows),
         out_shape=(
             jax.ShapeDtypeStruct((every, rows, LANES), jnp.float32),
             jax.ShapeDtypeStruct((2, 3 * rows, LANES), jnp.float32),
         ),
-        in_specs=[vmem],
+        in_specs=[smem, vmem, vmem],
         out_specs=(vmem, vmem),
         scratch_shapes=[
+            pltpu.VMEM((used, 2, cells, blocks, cy, LANES), source.dtype),
             pltpu.VMEM((2, used, 2, cells, blocks, cy, LANES), source.dtype),
             pltpu.VMEM((2, 3 * rows, LANES), jnp.float32),
             pltpu.SemaphoreType.DMA((2, used)),
@@ -255,7 +238,7 @@
         ],
         compiler_params=pltpu.CompilerParams(
             collective_id=0, has_side_effects=True, vmem_limit_bytes=32 << 20),
-    )(picked)
+    )(snap_index, source, receiver)
     return pl.pallas_call(
         functools.partial(image_kernel, lags, cell_rows),
         out_shape=jax.ShapeDtypeStruct((lags, cells, cy, nz), jnp.float32),

time: 31.3 us -> 31 us (level)
  Pallas kernels: 29.2 us -> 27.2 us
  local copies, waits for them, and re-layouts: 1.78 us -> 3.57 us
    pallas_call x1 -> x0, Pallas kernels: 2.84 us -> none  [local(): pl.pallas_call(functools.partial(pick_kernel, used), out_shape=jax.ShapeD...]
    unnamed x4 -> x8, local copies, waits for them, and re-layouts: 1.78 us -> 3.57 us
    pallas_call x1, Pallas kernels: 21.1 us -> 21.9 us  [local(): pl.pallas_call(functools.partial(exchange_kernel, tiles, cell_rows), out_...]
where the time goes in v3:
time: 31 us; the launch traced here: 30.7 us
  Pallas kernels  27.2 us (88%)
  local copies, waits for them, and re-layouts  3.57 us (12%)
    pallas_call x1, Pallas kernels, local(): pl.pallas_call(functools.partial(exchange_kernel, tiles, cell_rows), out_...  21.9 us
    pallas_call x1, Pallas kernels, local(): pl.pallas_call(functools.partial(image_kernel, lags, cell_rows), out_shap...  5.21 us
    unnamed x8, local copies, waits for them, and re-layouts  3.57 us

profile of v3, /device:TPU:9, one launch (start us, length us, event | category | flops | bytes accessed | tf_op | source)
XLA Modules:
  0.0 30.7 jit_solution(5820310964718863049)
XLA Ops:
  0.0 0.0 copy-start
  0.0 1.1 %copy-done = bf16[8,32,4,384]{3,2,1,0:T(4,128)(2,1)S(1)} copy-done((bf16[8,32,4,384]{3,2,1,0:T(4,128)(2,1)S(1)}, bf16[8,32,4,384]{3,2,1,0:T(4,128)(2,1)}, u32[]{:S(2)}) %copy-start) | copy-done | bytes 786456
  1.1 0.0 copy-start.1
  1.1 1.1 %copy-done.1 = bf16[8,32,4,384]{3,2,1,0:T(4,128)(2,1)S(1)} copy-done((bf16[8,32,4,384]{3,2,1,0:T(4,128)(2,1)S(1)}, bf16[8,32,4,384]{3,2,1,0:T(4,128)(2,1)}, u32[]{:S(2)}) %copy-start.1) | copy-done | bytes 786456
  2.3 0.0 copy-start.2
  2.3 0.7 %copy-done.2 = s32[4]{0:T(128)S(1)} copy-done((s32[4]{0:T(128)S(1)}, s32[4]{0:T(128)}, u32[]{:S(2)}) %copy-start.2) | copy-done | bytes 40
  2.9 21.9 %shard_map.46 = (f32[65,384,128]{2,1,0:T(8,128)S(1)}, f32[2,1152,128]{2,1,0:T(8,128)S(1)}) custom-call(s32[4]{0:T(128)S(1)} %copy-done.2, bf16[8,32,4,384]{3,2,1,0:T(4,128)(2,1)S(1)} %copy-done, bf16[8,32,4,384]{3,2,1,0:T(4,128)(2,1)S(1)} %copy-done.1), custom_call_target="tpu_custom_call" | custom-call | tf_op jit(solution)/shard_map/pallas_call | solution.py:224
  24.9 0.0 copy-start.3
  24.9 0.6 %copy-done.3 = s32[64]{0:T(128)S(1)} copy-done((s32[64]{0:T(128)S(1)}, s32[64]{0:T(128)}, u32[]{:S(2)}) %copy-start.3) | copy-done | bytes 280
  25.5 5.2 %shard_map.47 = f32[64,32,4,384]{3,2,1,0:T(4,128)} custom-call(s32[64]{0:T(128)S(1)} %copy-done.3, f32[65,384,128]{2,1,0:T(8,128)S(1)} %get-tuple-element.7.partial_ref, f32[2,1152,128]{2,1,0:T(8,128)S(1)} %get-tuple-element.8.last_ref), custom_call_target="tpu_custom_call" | custom-call | tf_op jit(solution)/shard_map/pallas_call | solution.py:242
Async XLA Ops:
  0.0 1.1 %copy-start = (bf16[8,32,4,384]{3,2,1,0:T(4,128)(2,1)S(1)}, bf16[8,32,4,384]{3,2,1,0:T(4,128)(2,1)}, u32[]{:S(2)}) copy-start(bf16[8,32,4,384]{3,2,1,0:T(4,128)(2,1)} %src_ref.1) | copy-start | bytes 2359300
  1.1 1.1 %copy-start.1 = (bf16[8,32,4,384]{3,2,1,0:T(4,128)(2,1)S(1)}, bf16[8,32,4,384]{3,2,1,0:T(4,128)(2,1)}, u32[]{:S(2)}) copy-start(bf16[8,32,4,384]{3,2,1,0:T(4,128)(2,1)} %rec_ref.1) | copy-start | bytes 2359300
  2.3 0.7 %copy-start.2 = (s32[4]{0:T(128)S(1)}, s32[4]{0:T(128)}, u32[]{:S(2)}) copy-start(s32[4]{0:T(128)} %snap_ref.1) | copy-start | bytes 52
  24.9 0.7 %copy-start.3 = (s32[64]{0:T(128)S(1)}, s32[64]{0:T(128)}, u32[]{:S(2)}) copy-start(s32[64]{0:T(128)} %offset_ref.1) | copy-start | bytes 772

commit v4 on v3

--- a/solution.py
+++ b/solution.py
@@ -196,14 +196,14 @@
                         image.at[index, :, block], out_ref.at[slot, :, :, lanes(block)], out_sem).start()
 
     def even_groups(number, carry):
-        group(3 * number - HMAX // 2, 0, 3)
+        group(11 * number - HMAX // 2, 0, 11)
         return carry
 
     def odd_groups(number, carry):
         group(4 * number - HMAX // 2, 1, 4)
         return carry
 
-    lax.fori_loop(0, (HMAX + 1) // 3, even_groups, 0)
+    lax.fori_loop(0, (HMAX + 1) // 11, even_groups, 0)
     lax.fori_loop(0, HMAX // 4, odd_groups, 0)
     for block in range(blocks):
         pltpu.make_async_copy(

time: 31 us -> 31.1 us (level)
  no operation moved by 1% of the time
where the time goes in v4:
time: 31.1 us; the launch traced here: 30.9 us
  Pallas kernels  27.3 us (88%)
  local copies, waits for them, and re-layouts  3.57 us (11%)
    pallas_call x1, Pallas kernels, local(): pl.pallas_call(functools.partial(exchange_kernel, tiles, cell_rows), out_...  21.9 us
    pallas_call x1, Pallas kernels, local(): pl.pallas_call(functools.partial(image_kernel, lags, cell_rows), out_shap...  5.36 us
    unnamed x8, local copies, waits for them, and re-layouts  3.57 us

profile of v4, /device:TPU:9, one launch (start us, length us, event | category | flops | bytes accessed | tf_op | source)
XLA Modules:
  0.0 30.9 jit_solution(5250042032027437084)
XLA Ops:
  0.0 0.0 copy-start
  0.0 1.1 %copy-done = bf16[8,32,4,384]{3,2,1,0:T(4,128)(2,1)S(1)} copy-done((bf16[8,32,4,384]{3,2,1,0:T(4,128)(2,1)S(1)}, bf16[8,32,4,384]{3,2,1,0:T(4,128)(2,1)}, u32[]{:S(2)}) %copy-start) | copy-done | bytes 786456
  1.1 0.0 copy-start.1
  1.1 1.1 %copy-done.1 = bf16[8,32,4,384]{3,2,1,0:T(4,128)(2,1)S(1)} copy-done((bf16[8,32,4,384]{3,2,1,0:T(4,128)(2,1)S(1)}, bf16[8,32,4,384]{3,2,1,0:T(4,128)(2,1)}, u32[]{:S(2)}) %copy-start.1) | copy-done | bytes 786456
  2.3 0.0 copy-start.2
  2.3 0.7 %copy-done.2 = s32[4]{0:T(128)S(1)} copy-done((s32[4]{0:T(128)S(1)}, s32[4]{0:T(128)}, u32[]{:S(2)}) %copy-start.2) | copy-done | bytes 40
  2.9 21.9 %shard_map.46 = (f32[65,384,128]{2,1,0:T(8,128)S(1)}, f32[2,1152,128]{2,1,0:T(8,128)S(1)}) custom-call(s32[4]{0:T(128)S(1)} %copy-done.2, bf16[8,32,4,384]{3,2,1,0:T(4,128)(2,1)S(1)} %copy-done, bf16[8,32,4,384]{3,2,1,0:T(4,128)(2,1)S(1)} %copy-done.1), custom_call_target="tpu_custom_call" | custom-call | tf_op jit(solution)/shard_map/pallas_call | solution.py:224
  24.9 0.0 copy-start.3
  24.9 0.6 %copy-done.3 = s32[64]{0:T(128)S(1)} copy-done((s32[64]{0:T(128)S(1)}, s32[64]{0:T(128)}, u32[]{:S(2)}) %copy-start.3) | copy-done | bytes 280
  25.5 5.4 %shard_map.47 = f32[64,32,4,384]{3,2,1,0:T(4,128)} custom-call(s32[64]{0:T(128)S(1)} %copy-done.3, f32[65,384,128]{2,1,0:T(8,128)S(1)} %get-tuple-element.7.partial_ref, f32[2,1152,128]{2,1,0:T(8,128)S(1)} %get-tuple-element.8.last_ref), custom_call_target="tpu_custom_call" | custom-call | tf_op jit(solution)/shard_map/pallas_call | solution.py:242
Async XLA Ops:
  0.0 1.1 %copy-start = (bf16[8,32,4,384]{3,2,1,0:T(4,128)(2,1)S(1)}, bf16[8,32,4,384]{3,2,1,0:T(4,128)(2,1)}, u32[]{:S(2)}) copy-start(bf16[8,32,4,384]{3,2,1,0:T(4,128)(2,1)} %src_ref.1) | copy-start | bytes 2359300
  1.1 1.1 %copy-start.1 = (bf16[8,32,4,384]{3,2,1,0:T(4,128)(2,1)S(1)}, bf16[8,32,4,384]{3,2,1,0:T(4,128)(2,1)}, u32[]{:S(2)}) copy-start(bf16[8,32,4,384]{3,2,1,0:T(4,128)(2,1)} %rec_ref.1) | copy-start | bytes 2359300
  2.3 0.7 %copy-start.2 = (s32[4]{0:T(128)S(1)}, s32[4]{0:T(128)}, u32[]{:S(2)}) copy-start(s32[4]{0:T(128)} %snap_ref.1) | copy-start | bytes 52
  24.9 0.7 %copy-start.3 = (s32[64]{0:T(128)S(1)}, s32[64]{0:T(128)}, u32[]{:S(2)}) copy-start(s32[64]{0:T(128)} %offset_ref.1) | copy-start | bytes 772
